TPU v7x, 128 devices: a whole 4x4x4 slice. The times are simulated.
128 devices in a mesh: row: 16 (over x, y), col: 8 (over z, core).
Axes of the slice: x: 4, y: 4, z: 4, core: 2. Of those that a mesh axis runs over, the one named last changes fastest.
Arguments:
- x_block: float32 [131072, 64], P(('col', 'row')), may hold values from -6 to 6
- r_block: float32 [131072, 64], P(('col', 'row')), may hold values from -6 to 6
- p_block: float32 [131072, 64], P(('col', 'row')), may hold values from -6 to 6
- neighbor_count: int32 [131072], P(('col', 'row')), may hold values from 8 to 32
- tile_values: bfloat16 [16, 8, 64, 128, 128], P('row', 'col'), may hold values from 0 to 0.079589844
- tile_row: int32 [16, 8, 64], P('row', 'col'), may hold values from 0 to 127
- tile_col: int32 [16, 8, 64], P('row', 'col'), may hold values from 0 to 63
- tile_count: int32 [16, 8], P('row', 'col'), may hold values from 16 to 64, as said below
Outputs:
- x_next: float32 [131072, 64], P(('col', 'row'))
- r_next: float32 [131072, 64], P(('col', 'row'))
- next_directions: float32 [131072, 64], P(('col', 'row'))
Inputs may be any that keep to these rules, and one draw needn't show every extreme that they name: `tile_count`: slots at or past a device's count hold no tile; some device holds exactly 64 live tiles.
All inputs are finite; a program needn't handle non-finite values.
Results may differ from a plain program's by a relative error of at most 0.0055.
Values may be sent and summed in bfloat16 or wider, within the bound.
A program may use at most 128 MiB of HBM per device.

v0:
```python
import jax
import jax.numpy as jnp
from jax import lax
from jax.sharding import PartitionSpec as P

ITERS = 2
RR_STEPS = 3


def small_product(left, right):
    return jnp.matmul(left, right, precision=lax.Precision.HIGHEST)


def ritz_step(gram_g, gram_h, width_k):
    lower = jnp.linalg.cholesky(gram_g)
    half_left = lax.linalg.triangular_solve(lower, gram_h, left_side=True, lower=True)
    reduced = lax.linalg.triangular_solve(
        lower, half_left, left_side=False, lower=True, transpose_a=True
    )
    reduced = 0.5 * (reduced + reduced.T)
    order = reduced.shape[0]
    offset_operator = reduced + 4.0 * jnp.eye(order, dtype=jnp.float32)
    basis = jnp.eye(order, dtype=jnp.float32)[:, :width_k]
    for inner in range(RR_STEPS):
        basis = small_product(offset_operator, basis)
        factor = jnp.linalg.cholesky(small_product(basis.T, basis))
        basis = lax.linalg.triangular_solve(
            factor, basis, left_side=False, lower=True, transpose_a=True
        )
    theta = small_product(basis.T, small_product(reduced, basis))
    coeffs = lax.linalg.triangular_solve(lower, basis, left_side=True, lower=True, transpose_a=True)
    return (coeffs, theta)


def per_device(
    x_block, r_block, p_block, neighbor_count, tile_values, tile_row, tile_col, tile_count
):
    row_processors = lax.axis_size("row")
    col_devices = lax.axis_size("col")
    row_count = x_block.shape[0]
    width_k = x_block.shape[1]
    tile_edge = tile_values.shape[3]
    node_total = float(row_count * row_processors * col_devices)
    tile_submatrix = tile_values[0, 0]
    live_slot = jnp.arange(tile_submatrix.shape[0]) < tile_count[0, 0]
    tile_submatrix = jnp.where(
        live_slot[:, None, None], tile_submatrix, jnp.zeros_like(tile_submatrix)
    )
    targets = tile_row[0, 0]
    source_nodes = tile_col[0, 0]
    degree_scale = (1.0 / jnp.sqrt(neighbor_count.astype(jnp.float32)))[:, None]
    basis_rows, resid_rows, search_rows = (x_block, r_block, p_block)
    for iteration in range(ITERS):
        block_panel = jnp.concatenate([basis_rows, resid_rows, search_rows], axis=1)
        panel_width = block_panel.shape[1]
        scaled = (degree_scale * block_panel).astype(jnp.bfloat16)
        gathered = lax.all_gather(scaled, "col", axis=0, tiled=True)
        block_list = gathered.reshape(-1, tile_edge, panel_width)
        selected_entries = jnp.take(block_list, source_nodes, axis=0)
        tile_contributions = jnp.einsum(
            "iks,isq->ikq", tile_submatrix, selected_entries, preferred_element_type=jnp.float32
        )
        partial_value = jax.ops.segment_sum(
            tile_contributions, targets, num_segments=row_processors * row_count // tile_edge
        )
        partial_value = partial_value.reshape(row_processors * row_count, panel_width)
        owned = lax.psum_scatter(partial_value, "row", scatter_dimension=0, tiled=True)
        image = degree_scale * owned
        gram_g, cross = lax.psum(
            (small_product(block_panel.T, block_panel), small_product(block_panel.T, image)),
            ("row", "col"),
        )
        gram_g = gram_g / node_total
        gram_h = (cross + cross.T) / (2.0 * node_total)
        coeffs, theta = ritz_step(gram_g, gram_h, width_k)
        search_coeffs = jnp.concatenate(
            [jnp.zeros((width_k, width_k), jnp.float32), coeffs[width_k:]], axis=0
        )
        basis_rows = small_product(block_panel, coeffs)
        resid_rows = small_product(image, coeffs) - small_product(basis_rows, theta)
        search_rows = small_product(block_panel, search_coeffs)
    return (basis_rows, resid_rows, search_rows)


def solution(mesh):
    placed = (
        P(("col", "row"), None),
        P(("col", "row"), None),
        P(("col", "row"), None),
        P(("col", "row")),
        P("row", "col", None, None, None),
        P("row", "col", None),
        P("row", "col", None),
        P("row", "col"),
    )
    return jax.shard_map(
        per_device,
        mesh=mesh,
        in_specs=placed,
        out_specs=(P(("col", "row"), None), P(("col", "row"), None), P(("col", "row"), None)),
        check_vma=False,
    )
```

profile of v0, /device:TPU:1, one launch (start us, length us, event | category | flops | bytes accessed | tf_op | source)
XLA Modules:
  0.0 854.4 jit_solution(5538530765643794953)
XLA Ops:
  7.9 1.0 constant_dynamic-update-slice_fusion.2
  8.9 1.0 constant_dynamic-update-slice_fusion.1
  12.4 31.0 %all-gather.3.cloned.1.call-done = bf16[8192,192]{0,1:T(8,128)(2,1)} async-done(((bf16[1024,192]{0,1:T(8,128)(2,1)}), bf16[8192,192]{0,1:T(8,128)(2,1)}) %all-gather.3.cloned.1.call-update) | async-done | bytes 3145744 | tf_op jit(solution)/shard_map/all_gather | solution.py:57
  43.4 4.5 copy_bitcast_fusion.3
  47.9 4.7 gather_fusion
  52.6 6.0 fusion.2
  58.6 6.2 broadcast.187.clone
  64.8 16.6 %scatter_fusion = f32[128,128,192]{1,2,0:T(8,128)} fusion(f32[128,128,192]{1,2,0:T(8,128)} %broadcast.187.clone, s32[64]{0:T(128)S(1)} %bitcast.240, f32[64,128,192]{1,2,0:T(8,128)} %fusion.2), kind=kCustom, calls=%fused_computation.2 | custom fusion | flops 1572864 | bytes 18874624 | tf_op jit(solution)/shard_map/scatter-add | solution.py:63
  81.4 10.5 %copy_bitcast_fusion.1 = f32[16384,192]{0,1:T(8,128)} fusion(f32[128,128,192]{1,2,0:T(8,128)} %scatter_fusion), kind=kLoop, calls=%fused_computation.5 | loop fusion | bytes 25165824 | tf_op jit(solution)/shard_map/reshape | solution.py:66
  92.0 1.5 fusion.139
  93.5 92.2 %reduce-scatter.3.cloned.1.call-done = f32[1024,192]{0,1:T(8,128)} async-done(((f32[16384,192]{0,1:T(8,128)}), f32[1024,192]{0,1:T(8,128)}) %reduce-scatter.3.cloned.1.call-update) | async-done | bytes 786448 | tf_op jit(solution)/shard_map/reduce_scatter | solution.py:67
  185.7 2.6 fusion.14
  188.6 146.2 %all-reduce.16.cloned.1.call-done = (f32[192,192]{1,0:T(8,128)}, f32[192,192]{0,1:T(8,128)}) async-done(((f32[192,192]{1,0:T(8,128)}, f32[192,192]{0,1:T(8,128)}), (f32[192,192]{1,0:T(8,128)}, f32[192,192]{0,1:T(8,128)})) %all-reduce.16.cloned.1.call-update) | async-done | bytes 294928 | tf_op jit(solution)/shard_map/psum | solution.py:69
  334.8 1.0 broadcast_multiply_fusion.1
  336.9 11.7 %cholesky.238 = f32[128,128]{1,0:T(8,128)S(1)} custom-call(f32[128,128]{1,0:T(8,128)S(1)} %cholesky.376), custom_call_target="Cholesky" | custom-call | tf_op jit(solution)/shard_map/jit(cholesky)/cholesky | solution.py:15
  348.6 9.8 %custom-call.31 = f32[1,128,128]{1,2,0:T(8,128)S(1)} custom-call(f32[1,128,128]{2,1,0:T(8,128)S(1)} %get-tuple-element.95), custom_call_target="InvertDiagBlocksLowerTriangular" | custom-call | tf_op jit(solution)/shard_map/jit(cholesky)/cholesky | solution.py:15
  358.8 5.8 cholesky.258
  367.4 20.1 %custom-call.37 = f32[2,128,128]{1,2,0:T(8,128)S(1)} custom-call(f32[2,128,128]{2,1,0:T(8,128)S(1)} %pad_maximum_fusion.3), custom_call_target="InvertDiagBlocksLowerTriangular" | custom-call | tf_op jit(solution)/shard_map/triangular_solve/custom-call.7 | solution.py:31
  390.6 5.8 cholesky.274
  397.8 4.9 custom-call.34
  403.6 5.8 cholesky.285
  410.8 4.9 custom-call.35
  416.6 5.8 cholesky.296
  423.8 4.9 custom-call.36
  433.4 26.9 %all-gather.5.cloned.1.call-done = bf16[8192,192]{0,1:T(8,128)(2,1)} async-done(((bf16[1024,192]{0,1:T(8,128)(2,1)}), bf16[8192,192]{0,1:T(8,128)(2,1)}) %all-gather.5.cloned.1.call-update) | async-done | bytes 3145744 | tf_op jit(solution)/shard_map/all_gather | solution.py:57
  460.3 2.8 copy_bitcast_fusion.2
  463.0 2.6 gather_fusion.1
  465.7 6.7 fusion
  472.3 6.2 broadcast.187
  478.5 16.6 %scatter_fusion.1 = f32[128,128,192]{1,2,0:T(8,128)} fusion(f32[128,128,192]{1,2,0:T(8,128)} %broadcast.187, s32[64]{0:T(128)S(1)} %bitcast.241, f32[64,128,192]{1,2,0:T(8,128)} %fusion), kind=kCustom, calls=%fused_computation.3 | custom fusion | flops 1572864 | bytes 18874624 | tf_op jit(solution)/shard_map/scatter-add | solution.py:63
  495.1 10.5 %copy_bitcast_fusion = f32[16384,192]{0,1:T(8,128)} fusion(f32[128,128,192]{1,2,0:T(8,128)} %scatter_fusion.1), kind=kLoop, calls=%fused_computation.4 | loop fusion | bytes 25165824 | tf_op jit(solution)/shard_map/reshape | solution.py:66
  506.6 1.5 fusion.138
  508.1 91.4 %reduce-scatter.5.cloned.1.call-done = f32[1024,192]{0,1:T(8,128)} async-done(((f32[16384,192]{0,1:T(8,128)}), f32[1024,192]{0,1:T(8,128)}) %reduce-scatter.5.cloned.1.call-update) | async-done | bytes 786448 | tf_op jit(solution)/shard_map/reduce_scatter | solution.py:67
  599.6 2.6 fusion.10
  602.2 146.2 %all-reduce.14.cloned.1.call-done = (f32[192,192]{0,1:T(8,128)}, f32[192,192]{0,1:T(8,128)}) async-done(((f32[192,192]{0,1:T(8,128)}, f32[192,192]{0,1:T(8,128)}), (f32[192,192]{0,1:T(8,128)}, f32[192,192]{0,1:T(8,128)})) %all-reduce.14.cloned.1.call-update) | async-done | bytes 294928 | tf_op jit(solution)/shard_map/psum | solution.py:69
  748.4 1.0 broadcast_multiply_fusion
  750.5 11.7 %cholesky.309 = f32[128,128]{1,0:T(8,128)S(1)} custom-call(f32[128,128]{1,0:T(8,128)S(1)} %cholesky.379), custom_call_target="Cholesky" | custom-call | tf_op jit(solution)/shard_map/jit(cholesky)/cholesky | solution.py:15
  762.2 9.8 %custom-call.38 = f32[1,128,128]{1,2,0:T(8,128)S(1)} custom-call(f32[1,128,128]{2,1,0:T(8,128)S(1)} %get-tuple-element.93), custom_call_target="InvertDiagBlocksLowerTriangular" | custom-call | tf_op jit(solution)/shard_map/jit(cholesky)/cholesky | solution.py:15
  772.4 5.8 cholesky.329
  781.1 19.9 %custom-call.44 = f32[2,128,128]{1,2,0:T(8,128)S(1)} custom-call(f32[2,128,128]{2,1,0:T(8,128)S(1)} %pad_maximum_fusion.4), custom_call_target="InvertDiagBlocksLowerTriangular" | custom-call | tf_op jit(solution)/shard_map/triangular_solve/custom-call.7 | solution.py:31
  804.0 5.8 cholesky.345
  811.2 4.9 custom-call.41
  817.0 5.8 cholesky.356
  824.2 4.9 custom-call.42
  830.0 5.8 cholesky.367
  837.2 4.9 custom-call.43
  843.3 1.3 fusion.57
  846.2 1.1 convolution_subtract_fusion
  (163 shorter events, 34.5 us)
Async XLA Ops:
  7.2 5.2 copy-start.11
  7.2 36.3 %all-gather.3.cloned.1.call-start = ((), (), s32[]{:S(2)}) async-start(), calls=%async_computation.2 | async-start | bytes 3538944 | tf_op jit(solution)/shard_map/all_gather | solution.py:57
  11.7 174.0 %reduce-scatter.3.cloned.1.call-start = ((), (), s32[]{:S(2)}) async-start(), calls=%async_computation.3 | async-start | bytes 13369344 | tf_op jit(solution)/shard_map/reduce_scatter | solution.py:67
  47.9 4.7 copy-start
  58.6 6.2 copy-start.10
  91.9 242.9 %all-reduce.16.cloned.1.call-start = ((), (), s32[]{:S(2)}) async-start(), calls=%async_computation.7 | async-start | bytes 786432 | tf_op jit(solution)/shard_map/psum | solution.py:69
  188.4 271.9 %all-gather.5.cloned.1.call-start = ((), (), s32[]{:S(2)}) async-start(), calls=%async_computation.4 | async-start | bytes 3538944 | tf_op jit(solution)/shard_map/all_gather | solution.py:57
  334.8 52.8 %copy-start.8 = (f32[192,192]{1,0:T(8,128)S(1)}, f32[192,192]{1,0:T(8,128)}, u32[]{:S(2)}) copy-start(f32[192,192]{1,0:T(8,128)} %get-tuple-element.90) | copy-start | bytes 442372
  389.9 41.4 %copy-start.6 = (f32[1024,192]{0,1:T(8,128)S(1)}, f32[1024,192]{0,1:T(8,128)}, u32[]{:S(2)}) copy-start(f32[1024,192]{0,1:T(8,128)} %reduce-scatter.3.cloned.1.call-done) | copy-start | bytes 2359300
  431.1 2.3 copy-start.1
  432.5 0.9 copy-start.3
  433.3 166.2 %reduce-scatter.5.cloned.1.call-start = ((), (), s32[]{:S(2)}) async-start(), calls=%async_computation.5 | async-start | bytes 13369344 | tf_op jit(solution)/shard_map/reduce_scatter | solution.py:67
  505.6 0.9 copy-start.2
  505.6 1.0 copy-start.4
  505.6 242.8 %all-reduce.14.cloned.1.call-start = ((), (), s32[]{:S(2)}) async-start(), calls=%async_computation.6 | async-start | bytes 786432 | tf_op jit(solution)/shard_map/psum | solution.py:69
  748.4 52.6 %copy-start.9 = (f32[192,192]{0,1:T(8,128)S(1)}, f32[192,192]{0,1:T(8,128)}, u32[]{:S(2)}) copy-start(f32[192,192]{0,1:T(8,128)} %get-tuple-element.88) | copy-start | bytes 442372
  803.4 42.1 %copy-start.5 = (f32[1024,192]{0,1:T(8,128)S(1)}, f32[1024,192]{0,1:T(8,128)}, u32[]{:S(2)}) copy-start(f32[1024,192]{0,1:T(8,128)} %reduce-scatter.5.cloned.1.call-done) | copy-start | bytes 2359300
  845.3 2.1 copy-start.7
Sparse Core Ops, SparseCore 0:
  11.8 31.5 all-gather.2
  92.0 93.6 reduce-scatter.2
  191.1 143.6 all-reduce.15
  433.5 26.7 all-gather.4
  505.7 93.7 reduce-scatter.4
  604.8 143.5 all-reduce.13
where the time goes:
time: 861 us; the launch traced here: 854 us
  waiting for transfers between devices  534 us (62%)
  other arithmetic  210 us (24%)
  local copies, waits for them, and re-layouts  52.8 us (6%)
  matrix products  38.8 us (5%)
  between operations  18.5 us (2%)
    psum x2, waiting for transfers between devices, per_device(): lax.psum((small_product(block_panel.T, block_panel), small_product(block_...  292 us
    reduce_scatter x2, waiting for transfers between devices, per_device(): lax.psum_scatter(partial_value, 'row', scatter_dimension=0, tiled=True)  184 us
    all_gather x2, waiting for transfers between devices, per_device(): gathered = lax.all_gather(scaled, 'col', axis=0, tiled=True)  57.9 us
    another operation x14, other arithmetic, ritz_step(): lower = jnp.linalg.cholesky(gram_g)  57.4 us
    another operation x10, other arithmetic, ritz_step(): lax.linalg.triangular_solve(lower, basis, left_side=True, lower=True, tra...  40.2 us
    another operation x18, other arithmetic, ritz_step(): factor = jnp.linalg.cholesky(small_product(basis.T, basis))  39.1 us
    another operation x12, other arithmetic, ritz_step(): lax.linalg.triangular_solve(factor, basis, left_side=False, lower=True, t...  33.3 us
    scatter-add x2, other arithmetic, per_device(): jax.ops.segment_sum(tile_contributions, targets, num_segments=row_process...  33.2 us
  transfers between devices with their start and end apart: 6, of which 6 were waited for; matrix products, arithmetic and copies ran while one was open for 0% of the time, Pallas kernels for 0%

commit v1 on v0

v1 whole, which is shorter than its diff:
```python
import functools

import jax
import jax.numpy as jnp
from jax import lax
from jax.experimental import pallas as pl
from jax.experimental.pallas import tpu as pltpu
from jax.sharding import PartitionSpec as P

ITERS = 2
RR_STEPS = 3
K = 64
W3 = 3 * K
TILE = 128
BLOCKS = 8
SLOTS = 64
ROWS = 16
COLS = 8
SIDE = 4
NODES = BLOCKS * TILE
NODE_TOTAL = NODES * ROWS * COLS
F32 = jnp.float32
BF16 = jnp.bfloat16
MESH = pl.DeviceIdType.MESH
PIVOT_FLOOR = 1.0 / 64.0


def dot_nn(a, b):
    return lax.dot_general(
        a, b, (((1,), (0,)), ((), ())), precision=lax.Precision.HIGHEST, preferred_element_type=F32
    )


def dot_nt(a, b):
    return lax.dot_general(
        a, b, (((1,), (1,)), ((), ())), precision=lax.Precision.HIGHEST, preferred_element_type=F32
    )


def dot_tn(a, b):
    return lax.dot_general(
        a, b, (((0,), (0,)), ((), ())), precision=lax.Precision.HIGHEST, preferred_element_type=F32
    )


def eye(n):
    return jnp.where(
        lax.broadcasted_iota(jnp.int32, (n, n), 0) == lax.broadcasted_iota(jnp.int32, (n, n), 1), 1.0, 0.0
    ).astype(F32)


def inverse_factor(a):
    n = K
    both = jnp.concatenate([a, eye(n)], axis=1)
    tiles = [both[8 * t : 8 * t + 8, :] for t in range(n // 8)]
    sub = lax.broadcasted_iota(jnp.int32, (8, 2 * n), 0)
    for k in range(n):
        t0, kk = divmod(k, 8)
        row = tiles[t0][kk : kk + 1, :]
        scaled = row * (1.0 / row[:, k : k + 1])
        scaled = jnp.broadcast_to(scaled, (8, 2 * n))
        for t in range(t0, n // 8):
            col = jnp.broadcast_to(tiles[t][:, k : k + 1], (8, 2 * n))
            if t == t0:
                col = jnp.where(sub > kk, col, 0.0)
            tiles[t] = tiles[t] - col * scaled
    done = jnp.concatenate(tiles, axis=0)
    mask = eye(n)
    pivots = jnp.sum(done[:, :n] * mask, axis=1, keepdims=True)
    start = jnp.sum(a * mask, axis=1, keepdims=True)
    ratio = jnp.min(pivots / start)
    return done[:, n:] * lax.rsqrt(pivots), ratio


def main_kernel(first, width, center, *refs):
    vrows = width + 16 if center else width
    quarter = width // 4
    if first:
        x_ref, r_ref, p_ref, nc_ref, tiles_hbm, col_ref, link_ref = refs[:7]
        st_ref, ast_ref, h_ref, k_ref = refs[7:11]
        rest = refs[11:]
    else:
        st_ref, axp_ref, nc_ref, tiles_hbm, col_ref, link_ref = refs[:6]
        ast_ref, h_ref, k_ref = refs[6:9]
        rest = refs[9:]
    (
        tiles, vbuf, acc, sb, f1, n1, c1, tb, own, f2, n2, c2, part, ga, gb, gc, ha, hb, rsend, rrecv,
        load_sem, ag_s, ag_r, rs_s, rs_r, g_s, g_r, h_s, h_r, m_s, m_r,
    ) = rest

    row, col = lax.axis_index("row"), lax.axis_index("col")
    x, y = row // SIDE, lax.rem(row, SIDE)
    z, core = col // 2, lax.rem(col, 2)

    load = pltpu.make_async_copy(tiles_hbm, tiles, load_sem)
    load.start()

    barrier = pltpu.get_barrier_semaphore()
    for o in range(1, ROWS):
        pl.semaphore_signal(barrier, inc=1, device_id=(lax.rem(row + o, ROWS), col), device_id_type=MESH)
    for o in range(1, COLS):
        pl.semaphore_signal(barrier, inc=1, device_id=(row, lax.rem(col + o, COLS)), device_id_type=MESH)

    def remote(src, dst, ss, rs, where):
        return pltpu.make_async_remote_copy(
            src_ref=src, dst_ref=dst, send_sem=ss, recv_sem=rs, device_id=where, device_id_type=MESH
        )

    scale = 1.0 / jnp.sqrt(nc_ref[...].astype(F32))

    if first:
        for b in range(BLOCKS):
            at = pl.ds(b * TILE, TILE)
            st_ref[0:K, at] = jnp.transpose(x_ref[at, :])
            st_ref[K : 2 * K, at] = jnp.transpose(r_ref[at, :])
            st_ref[2 * K : W3, at] = jnp.transpose(p_ref[at, :])
    for b in range(BLOCKS):
        at = pl.ds(b * TILE, TILE)
        d_b = scale[b : b + 1, :]
        if first:
            vbuf[col, b, 0:width, :] = (st_ref[:, at] * d_b).astype(BF16)
        else:
            vbuf[col, b, 0:width, :] = (st_ref[K : 2 * K, at] * d_b).astype(BF16)
        if center:
            sub = lax.broadcasted_iota(jnp.int32, (16, TILE), 0)
            vbuf[col, b, width : width + 16, :] = jnp.where(sub == 0, d_b, 0.0).astype(BF16)

    pl.semaphore_wait(barrier, ROWS - 1 + COLS - 1)

    up = (row, lax.rem(z + 1, SIDE) * 2 + core)
    down = (row, lax.rem(z + 3, SIDE) * 2 + core)
    mate = (row, z * 2 + 1 - core)
    low, high = pl.ds(0, BLOCKS // 2), pl.ds(BLOCKS // 2, BLOCKS // 2)

    def gather(n, src, where):
        cp = remote(src, src, ag_s.at[n], ag_r.at[n], where)
        cp.start()
        return cp

    mine = vbuf.at[col]
    ag = {}
    ag[0] = gather(0, mine, up)
    ag[1] = gather(1, mine, down)
    ag[2] = gather(2, mine, mate)

    def pack(full):
        for c in range(W3 // 32):
            part[c] = full[32 * c : 32 * c + 32, 0:TILE]
        for c in range(2):
            part[6 + c] = jnp.zeros((32, TILE), F32)
            part[6 + c, :, 0:K] = full[2 * K + 32 * c : 2 * K + 32 * c + 32, TILE : TILE + K]

    def reduce_send(buf, ss, rs):
        buf[col] = part[col]
        cps = []
        for o in range(1, COLS):
            to = lax.rem(col + o, COLS)
            cp = remote(part.at[to], buf.at[col], ss.at[o - 1], rs.at[o - 1], (row, to))
            cp.start()
            cps.append(cp)
        return cps

    def reduce_cross(cps, buf, buf2, ss, rs):
        for cp in cps:
            cp.wait_recv()
        total = buf[0]
        for c in range(1, COLS):
            total = total + buf[c]
        buf2[row] = total
        cps2 = []
        for o in range(1, ROWS):
            to = lax.rem(row + o, ROWS)
            cp = remote(buf2.at[row], buf2.at[row], ss.at[6 + o], rs.at[6 + o], (to, col))
            cp.start()
            cps2.append(cp)
        return cps2

    def reduce_share(cps, buf2, out, ss, rs):
        for cp in cps:
            cp.wait_recv()
        total = buf2[0]
        for c in range(1, ROWS):
            total = total + buf2[c]
        out[col] = total
        cps2 = []
        for o in range(1, COLS):
            to = lax.rem(col + o, COLS)
            cp = remote(out.at[col], out.at[col], ss.at[21 + o], rs.at[21 + o], (row, to))
            cp.start()
            cps2.append(cp)
        return cps2

    stv = st_ref[...]
    pack(dot_nt(stv, stv))
    g1 = reduce_send(ga, g_s, g_r)

    ag[0].wait_recv()
    below = lax.rem(z + 3, SIDE) * 2 + core
    ag[3] = gather(3, vbuf.at[below, low], up)
    ag[4] = gather(4, vbuf.at[below], mate)
    ag[1].wait_recv()
    above = lax.rem(z + 1, SIDE) * 2 + core
    ag[5] = gather(5, vbuf.at[above, high], down)
    ag[6] = gather(6, vbuf.at[above], mate)

    g2 = reduce_cross(g1, ga, gb, g_s, g_r)

    across = lax.rem(z + 2, SIDE) * 2 + core
    ag[3].wait_recv()
    ag[7] = gather(7, vbuf.at[across, low], mate)
    ag[5].wait_recv()
    ag[8] = gather(8, vbuf.at[across, high], mate)

    g3 = reduce_share(g2, gb, gc, g_s, g_r)

    for n in (2, 4, 6, 7, 8):
        ag[n].wait_recv()
    load.wait()

    acc[SLOTS] = jnp.zeros((vrows, TILE), F32)

    def tile_step(t, carry):
        products = []
        for u in range(2):
            s = 2 * t + u
            c = col_ref[s]
            products.append(
                lax.dot_general(
                    vbuf[c // BLOCKS, lax.rem(c, BLOCKS)],
                    tiles[s],
                    (((1,), (1,)), ((), ())),
                    preferred_element_type=F32,
                )
            )
        for u in range(2):
            s = 2 * t + u
            acc[s] = products[u] + acc[link_ref[s]]
        return carry

    lax.fori_loop(0, SLOTS // 2, tile_step, 0)

    if center:
        ones = jnp.ones((TILE, TILE), BF16)
        total = jnp.zeros((vrows, TILE), F32)
        for j in range(COLS):
            for b in range(BLOCKS):
                total = total + lax.dot_general(
                    vbuf[j, b], ones, (((1,), (1,)), ((), ())), preferred_element_type=F32
                )
        mean = total[0:width, :] / total[width : width + 1, :]
        mean_row = jnp.transpose(mean[0:TILE, :])[0:1, :]
        mean_row2 = jnp.transpose(jnp.concatenate([mean[TILE:width, :], jnp.zeros((2 * TILE - width, TILE), F32)], axis=0))[0:1, :]

    def place_step(t, carry):
        dx, dy, b = t // (SIDE * BLOCKS), lax.rem(t // BLOCKS, SIDE), lax.rem(t, BLOCKS)
        block = acc[link_ref[SLOTS + t]]
        if center:
            rsend[dx * SIDE + dy, pl.ds(b, 1), :] = block[width : width + 1, :]
            block = block[0:width, :] - mean * block[width : width + 1, :]
        block = block.astype(BF16)
        for q in range(4):
            piece = block[q * quarter : (q + 1) * quarter, :]
            if q < 2:
                sb[q, dx, dy, b] = piece
            else:
                sb[q, dy, dx, b] = piece
        return carry

    lax.fori_loop(0, ROWS * BLOCKS, place_step, 0)

    def neighbour(axis, step):
        if axis == 0:
            return (lax.rem(x + step + SIDE, SIDE) * SIDE + y, col)
        return (x * SIDE + lax.rem(y + step + SIDE, SIDE), col)

    place = (x, y)

    def at(axis, step):
        return lax.rem(place[axis] + step + SIDE, SIDE)

    phases = []
    for q in range(4):
        axis, sign = q // 2, 1 - 2 * (q % 2)
        cp = remote(sb.at[q, at(axis, 2)], f1.at[q], rs_s.at[q], rs_r.at[q], neighbour(axis, sign))
        cp.start()
        phases.append([cp])
    for q in range(4):
        axis, sign = q // 2, 1 - 2 * (q % 2)
        cp = remote(sb.at[q, at(axis, -sign)], n1.at[q], rs_s.at[4 + q], rs_r.at[4 + q], neighbour(axis, -sign))
        cp.start()
        phases[q].append(cp)

    mcps = []
    if center:
        for i in range(ROWS):
            rsend[i, 8:9, :] = mean_row
            rsend[i, 9:10, :] = mean_row2
            rsend[i, 10:16, :] = jnp.zeros((6, TILE), F32)
        rrecv[row] = rsend[row]
        for o in range(1, ROWS):
            to = lax.rem(row + o, ROWS)
            cp = remote(rsend.at[to], rrecv.at[row], m_s.at[o - 1], m_r.at[o - 1], (to, col))
            cp.start()
            mcps.append(cp)

    for cp in g3:
        cp.wait_recv()

    def gram(r, c):
        if (r, c) == (2, 2):
            return jnp.concatenate([gc[6, :, 0:K], gc[7, :, 0:K]], axis=0) * (1.0 / NODE_TOTAL)
        return jnp.concatenate(
            [gc[2 * r, :, c * K : c * K + K], gc[2 * r + 1, :, c * K : c * K + K]], axis=0
        ) * (1.0 / NODE_TOTAL)

    k11, unused = inverse_factor(gram(0, 0))
    l21 = dot_nt(gram(1, 0), k11)
    s22 = gram(1, 1) - dot_nt(l21, l21)
    l31 = dot_nt(gram(2, 0), k11)
    k_ref[...] = jnp.zeros((W3, W3), F32)
    k_ref[0:K, 0:K] = k11

    for q in range(4):
        axis, sign = q // 2, 1 - 2 * (q % 2)
        phases[q][0].wait_recv()
        to = at(axis, sign)

        def meet(t, carry, q=q, to=to):
            d2, b = t // BLOCKS, lax.rem(t, BLOCKS)
            sb[q, to, d2, b] = (sb[q, to, d2, b].astype(F32) + f1[q, d2, b].astype(F32)).astype(BF16)
            return carry

        lax.fori_loop(0, SIDE * BLOCKS, meet, 0)
        cp = remote(sb.at[q, to], c1.at[q], rs_s.at[8 + q], rs_r.at[8 + q], neighbour(axis, sign))
        cp.start()
        phases[q].append(cp)

    k22, unused = inverse_factor(s22)
    k21 = -dot_nn(k22, dot_nn(l21, k11))
    l32 = dot_nt(gram(2, 1) - dot_nt(l31, l21), k22)
    s33 = gram(2, 2) - dot_nt(l31, l31) - dot_nt(l32, l32)
    k_ref[K : 2 * K, 0:K] = k21
    k_ref[K : 2 * K, K : 2 * K] = k22

    second = []
    for q in range(4):
        axis, sign = q // 2, 1 - 2 * (q % 2)
        phases[q][1].wait_recv()
        phases[q][2].wait_recv()
        me = place[axis]

        def merge(t, carry, q=q, me=me):
            d2, b = t // BLOCKS, lax.rem(t, BLOCKS)
            total = sb[q, me, d2, b].astype(F32) + n1[q, d2, b].astype(F32) + c1[q, d2, b].astype(F32)
            tb[q, d2, b] = total.astype(BF16)
            return carry

        lax.fori_loop(0, SIDE * BLOCKS, merge, 0)
        axis = 1 - axis
        cp = remote(tb.at[q, at(axis, 2)], f2.at[q], rs_s.at[12 + q], rs_r.at[12 + q], neighbour(axis, sign))
        cp.start()
        cp2 = remote(tb.at[q, at(axis, -sign)], n2.at[q], rs_s.at[16 + q], rs_r.at[16 + q], neighbour(axis, -sign))
        cp2.start()
        second.append([cp, cp2])
    for q in range(4):
        axis, sign = 1 - q // 2, 1 - 2 * (q % 2)
        second[q][0].wait_recv()
        to = at(axis, sign)

        def meet2(b, carry, q=q, to=to):
            tb[q, to, b] = (tb[q, to, b].astype(F32) + f2[q, b].astype(F32)).astype(BF16)
            return carry

        lax.fori_loop(0, BLOCKS, meet2, 0)
        cp = remote(tb.at[q, to], c2.at[q], rs_s.at[20 + q], rs_r.at[20 + q], neighbour(axis, sign))
        cp.start()
        second[q].append(cp)

    k33, unused = inverse_factor(s33)
    k32 = -dot_nn(k33, dot_nn(l32, k22))
    k31 = -dot_nn(k33, dot_nn(l31, k11) + dot_nn(l32, k21))
    k_ref[2 * K : W3, 0:K] = k31
    k_ref[2 * K : W3, K : 2 * K] = k32
    k_ref[2 * K : W3, 2 * K : W3] = k33

    if center:
        for cp in mcps:
            cp.wait_recv()
        means = jnp.concatenate([rrecv[:, 8, :], rrecv[:, 9, :]], axis=1)
        weights = jnp.concatenate([rrecv[:, b, :] for b in range(BLOCKS)], axis=1)
        back = dot_tn(means, weights)

    for q in range(4):
        me = place[1 - q // 2]
        second[q][1].wait_recv()
        second[q][2].wait_recv()
        for b in range(BLOCKS):
            total = tb[q, me, b].astype(F32) + n2[q, b].astype(F32) + c2[q, b].astype(F32)
            if center:
                total = total + back[q * quarter : (q + 1) * quarter, b * TILE : (b + 1) * TILE]
            total = total * scale[b : b + 1, :]
            base = q * quarter if first else K + q * quarter
            ast_ref[base : base + quarter, b * TILE : (b + 1) * TILE] = total
    if not first:
        ast_ref[0:K, :] = axp_ref[0:K, :]
        ast_ref[2 * K : W3, :] = axp_ref[K : 2 * K, :]

    for cp in g1:
        cp.wait_send()
    astv = ast_ref[...]
    pack(0.5 * (dot_nt(stv, astv) + dot_nt(astv, stv)))
    h1 = reduce_send(ha, h_s, h_r)
    h2 = reduce_cross(h1, ha, hb, h_s, h_r)
    h3 = reduce_share(h2, hb, h_ref, h_s, h_r)
    for cp in h3:
        cp.wait_recv()

    for n in range(9):
        ag[n].wait_send()
    for cps in phases + second + [mcps, g2, g3, h1, h2, h3]:
        for cp in cps:
            cp.wait_send()


def main_call(first, width, center, operands, collective_id):
    vrows = width + 16 if center else width
    quarter = width // 4
    vmem = pl.BlockSpec(memory_space=pltpu.VMEM)
    smem = pl.BlockSpec(memory_space=pltpu.SMEM)
    hbm = pl.BlockSpec(memory_space=pl.ANY)
    lead = [vmem] * (4 if first else 3)
    shapes = [
        jax.ShapeDtypeStruct((W3, NODES), F32),
        jax.ShapeDtypeStruct((COLS, 32, TILE), F32),
        jax.ShapeDtypeStruct((W3, W3), F32),
    ]
    if first:
        shapes = [jax.ShapeDtypeStruct((W3, NODES), F32)] + shapes
    dma = pltpu.SemaphoreType.DMA
    scratch = [
        pltpu.VMEM((SLOTS, TILE, TILE), BF16),
        pltpu.VMEM((COLS, BLOCKS, vrows, TILE), BF16),
        pltpu.VMEM((SLOTS + 1, vrows, TILE), F32),
        pltpu.VMEM((4, SIDE, SIDE, BLOCKS, quarter, TILE), BF16),
        pltpu.VMEM((4, SIDE, BLOCKS, quarter, TILE), BF16),
        pltpu.VMEM((4, SIDE, BLOCKS, quarter, TILE), BF16),
        pltpu.VMEM((4, SIDE, BLOCKS, quarter, TILE), BF16),
        pltpu.VMEM((4, SIDE, BLOCKS, quarter, TILE), BF16),
        pltpu.VMEM((8, TILE), F32),
        pltpu.VMEM((4, BLOCKS, quarter, TILE), BF16),
        pltpu.VMEM((4, BLOCKS, quarter, TILE), BF16),
        pltpu.VMEM((4, BLOCKS, quarter, TILE), BF16),
        pltpu.VMEM((COLS, 32, TILE), F32),
        pltpu.VMEM((COLS, 32, TILE), F32),
        pltpu.VMEM((ROWS, 32, TILE), F32),
        pltpu.VMEM((COLS, 32, TILE), F32),
        pltpu.VMEM((COLS, 32, TILE), F32),
        pltpu.VMEM((ROWS, 32, TILE), F32),
        pltpu.VMEM((ROWS, 16, TILE), F32),
        pltpu.VMEM((ROWS, 16, TILE), F32),
        dma(()),
        dma((9,)),
        dma((9,)),
        dma((24,)),
        dma((24,)),
        dma((29,)),
        dma((29,)),
        dma((29,)),
        dma((29,)),
        dma((15,)),
        dma((15,)),
    ]
    return pl.pallas_call(
        functools.partial(main_kernel, first, width, center),
        name="operator_first" if first else "operator_next",
        out_shape=shapes,
        in_specs=lead + [hbm, smem, smem] if first else [vmem, vmem, vmem, hbm, smem, smem],
        out_specs=[vmem] * len(shapes),
        scratch_shapes=scratch,
        compiler_params=pltpu.CompilerParams(
            collective_id=collective_id, has_side_effects=True, vmem_limit_bytes=56 << 20
        ),
    )(*operands)


def full_symmetric(h_ref):
    left = jnp.concatenate([h_ref[c] for c in range(6)], axis=0)
    corner = jnp.concatenate([h_ref[6, :, 0:K], h_ref[7, :, 0:K]], axis=0)
    right = jnp.concatenate([jnp.transpose(left[TILE:W3, :]), corner], axis=0)
    return jnp.concatenate([left, right], axis=1) * (1.0 / NODE_TOTAL)


def ritz_kernel(last, *refs):
    h_ref, k_ref, st_ref, ast_ref = refs[:4]
    basis_t = refs[-1]
    outs = refs[4:-1]
    kinv = k_ref[...]
    reduced = dot_nt(dot_nn(kinv, full_symmetric(h_ref)), kinv)
    reduced = 0.5 * (reduced + jnp.transpose(reduced))
    shifted = reduced + 4.0 * eye(W3)

    power = shifted[0:K, :]
    for inner in range(RR_STEPS - 1):
        power = dot_nn(power, shifted)
    factor, ratio = inverse_factor(dot_nt(power, power))
    basis_t[...] = dot_nn(factor, power)

    @pl.when(jnp.logical_not(ratio > PIVOT_FLOOR))
    def stepwise():
        basis_t[...] = eye(W3)[0:K, :]

        def step(t, carry):
            moved = dot_nn(basis_t[...], shifted)
            inverse, unused = inverse_factor(dot_nt(moved, moved))
            basis_t[...] = dot_nn(inverse, moved)
            return carry

        lax.fori_loop(0, RR_STEPS, step, 0)

    z_t = basis_t[...]
    theta = dot_nt(dot_nn(z_t, reduced), z_t)
    c_t = dot_nn(z_t, kinv)
    lane = lax.broadcasted_iota(jnp.int32, (K, W3), 1)
    cp_t = jnp.where(lane < K, 0.0, c_t)
    drop_t = dot_tn(theta, c_t)
    stv, astv = st_ref[...], ast_ref[...]
    left = dot_nn(jnp.concatenate([c_t, cp_t, drop_t], axis=0), stv)
    if last:
        resid = dot_nn(c_t, astv) - left[2 * K : W3, :]
        for b in range(BLOCKS):
            lanes = slice(b * TILE, (b + 1) * TILE)
            at = pl.ds(b * TILE, TILE)
            outs[0][at, :] = jnp.transpose(left[0:K, lanes])
            outs[1][at, :] = jnp.transpose(resid[:, lanes])
            outs[2][at, :] = jnp.transpose(left[K : 2 * K, lanes])
    else:
        image = dot_nn(jnp.concatenate([c_t, cp_t], axis=0), astv)
        outs[0][0:K, :] = left[0:K, :]
        outs[0][K : 2 * K, :] = image[0:K, :] - left[2 * K : W3, :]
        outs[0][2 * K : W3, :] = left[K : 2 * K, :]
        outs[1][...] = image


def ritz_call(last, h, kinv, st, ast):
    vmem = pl.BlockSpec(memory_space=pltpu.VMEM)
    if last:
        shapes = [jax.ShapeDtypeStruct((NODES, K), F32)] * 3
    else:
        shapes = [jax.ShapeDtypeStruct((W3, NODES), F32), jax.ShapeDtypeStruct((2 * K, NODES), F32)]
    return pl.pallas_call(
        functools.partial(ritz_kernel, last),
        name="ritz_last" if last else "ritz",
        out_shape=shapes,
        in_specs=[vmem] * 4,
        out_specs=[vmem] * len(shapes),
        scratch_shapes=[pltpu.VMEM((K, W3), F32)],
        compiler_params=pltpu.CompilerParams(vmem_limit_bytes=32 << 20),
    )(h, kinv, st, ast)


def per_device(
    x_block, r_block, p_block, neighbor_count, tile_values, tile_row, tile_col, tile_count
):
    tiles = tile_values[0, 0]
    targets = tile_row[0, 0]
    counts = neighbor_count.reshape(BLOCKS, TILE)
    slot = jnp.arange(SLOTS, dtype=jnp.int32)
    wanted = jnp.concatenate([targets, jnp.arange(ROWS * BLOCKS, dtype=jnp.int32)])
    before = jnp.concatenate([slot, jnp.full((ROWS * BLOCKS,), SLOTS, jnp.int32)])
    live = (slot < tile_count[0, 0])[None, :]
    found = (wanted[:, None] == targets[None, :]) & live & (slot[None, :] < before[:, None])
    link = jnp.max(jnp.where(found, slot[None, :], -1), axis=1)
    link = jnp.where(link < 0, SLOTS, link)
    st, ast, h, kinv = main_call(
        True, W3, True, (x_block, r_block, p_block, counts, tiles, tile_col[0, 0], link), 0
    )
    st, axp = ritz_call(False, h, kinv, st, ast)
    ast, h, kinv = main_call(False, K, False, (st, axp, counts, tiles, tile_col[0, 0], link), 1)
    return tuple(ritz_call(True, h, kinv, st, ast))


def solution(mesh):
    placed = (
        P(("col", "row"), None),
        P(("col", "row"), None),
        P(("col", "row"), None),
        P(("col", "row")),
        P("row", "col", None, None, None),
        P("row", "col", None),
        P("row", "col", None),
        P("row", "col"),
    )
    return jax.shard_map(
        per_device,
        mesh=mesh,
        in_specs=placed,
        out_specs=(P(("col", "row"), None), P(("col", "row"), None), P(("col", "row"), None)),
        check_vma=False,
    )
```

time: 861 us -> 226 us (0.26)
  waiting for transfers between devices: 534 us -> 0 us
  other arithmetic: 210 us -> 2.09 us
  Pallas kernels: 0 us -> 204 us
  matrix products: 38.8 us -> 0 us
  local copies, waits for them, and re-layouts: 52.8 us -> 17.2 us
  between operations: 18.5 us -> 1.36 us
    psum x2 -> x0, waiting for transfers between devices: 292 us -> none  [per_device(): lax.psum((small_product(block_panel.T, block_panel), small_product(block_...]
    pallas_call x0 -> x4, Pallas kernels: none -> 204 us  [the longest x2 185 us: main_call(): pl.pallas_call(functools.partial(main_kernel, first, width, center), name...]
    reduce_scatter x2 -> x0, waiting for transfers between devices: 184 us -> none  [per_device(): lax.psum_scatter(partial_value, 'row', scatter_dimension=0, tiled=True)]
    another operation x56 -> x0, other arithmetic: 170 us -> none  [the longest x14 57.4 us: ritz_step(): lower = jnp.linalg.cholesky(gram_g)]
    all_gather x2 -> x0, waiting for transfers between devices: 57.9 us -> none  [per_device(): gathered = lax.all_gather(scaled, 'col', axis=0, tiled=True)]
    scatter-add x2 -> x0, other arithmetic: 33.2 us -> none  [per_device(): jax.ops.segment_sum(tile_contributions, targets, num_segments=row_process...]
    dot_general x30 -> x0, matrix products: 31.2 us -> none  [the longest x28 18.5 us: small_product(): return jnp.matmul(left, right, precision=lax.Precision.HIGHEST)]
    reshape x4 -> x0, local copies, waits for them, and re-layouts: 28.2 us -> none  [the longest x2 21 us: per_device(): partial_value.reshape(row_processors * row_count, panel_width)]
  transfers between devices with their start and end apart: 6 -> 0, of which waited for: 6 -> 0; matrix products, arithmetic and copies ran while one was open for 0% -> 0% of each run, Pallas kernels for 0% -> 0%
where the time goes in v1:
time: 226 us; the launch traced here: 225 us
  Pallas kernels  204 us (90%)
  local copies, waits for them, and re-layouts  17.2 us (8%)
    pallas_call x2, Pallas kernels, main_call(): pl.pallas_call(functools.partial(main_kernel, first, width, center), name...  185 us
    pallas_call x2, Pallas kernels, ritz_call(): pl.pallas_call(functools.partial(ritz_kernel, last), name='ritz_last' if...  19.3 us
    unnamed x23, local copies, waits for them, and re-layouts  14.6 us

profile of v1, /device:TPU:1, one launch (start us, length us, event | category | flops | bytes accessed | tf_op | source)
XLA Modules:
  0.0 225.0 jit_solution(15954836688862085664)
XLA Ops:
  1.3 0.7 pad_add_fusion
  2.0 0.8 select_reduce_fusion
  2.8 0.6 compare_select_fusion.refs_6_.refs_5_
  3.4 1.9 copy.17.refs_0_
  5.3 1.9 copy.18.refs_1_
  7.3 2.0 copy.19.refs_2_
  9.2 110.1 %operator_first.1 = (f32[192,1024]{1,0:T(8,128)}, f32[192,1024]{1,0:T(8,128)}, f32[8,32,128]{2,1,0:T(8,128)}, f32[192,192]{1,0:T(8,128)}) custom-call(f32[1024,64]{1,0:T(8,128)} %copy.17.refs_0_, f32[1024,64]{1,0:T(8,128)} %copy.18.refs_1_, f32[1024,64]{1,0:T(8,128)} %copy.19.refs_2_, s32[8,128]{1,0:T(8,128)} %bitcast.8, bf16[64,128,128]{2,1,0:T(8,128)(2,1)} %bitcast.6, ...), custom_call_target="tpu_custom_call" | custom-call | tf_op jit(solution)/shard_map/operator_first/pallas_call | solution.py:473
  119.4 0.0 copy-start.2
  119.4 1.1 copy-done.2
  120.5 0.0 copy-start.3
  120.5 1.1 copy-done.3
  121.6 0.0 copy-start.6
  121.7 0.9 copy-done.6
  122.6 0.0 copy-start.8
  122.6 0.9 copy-done.8
  123.5 9.6 %ritz.1 = (f32[192,1024]{1,0:T(8,128)S(1)}, f32[128,1024]{1,0:T(8,128)S(1)}) custom-call(f32[8,32,128]{2,1,0:T(8,128)S(1)} %copy-done.8, f32[192,192]{1,0:T(8,128)S(1)} %copy-done.6, f32[192,1024]{1,0:T(8,128)S(1)} %copy-done.2, f32[192,1024]{1,0:T(8,128)S(1)} %copy-done.3), custom_call_target="tpu_custom_call" | custom-call | tf_op jit(solution)/shard_map/ritz/pallas_call | solution.py:550
  133.0 0.0 copy-start
  133.1 0.9 copy-done
  133.9 0.0 copy-start.5
  133.9 0.8 copy-done.5
  134.7 0.0 copy-start.1
  134.7 74.9 %operator_next.1 = (f32[192,1024]{1,0:T(8,128)}, f32[8,32,128]{2,1,0:T(8,128)}, f32[192,192]{1,0:T(8,128)}) custom-call(f32[192,1024]{1,0:T(8,128)} %copy-done, f32[128,1024]{1,0:T(8,128)} %copy-done.5, s32[8,128]{1,0:T(8,128)} %bitcast.9, bf16[64,128,128]{2,1,0:T(8,128)(2,1)} %bitcast.7, s32[64]{0:T(128)} %bitcast.13, s32[192]{0:T(256)} %compare_select_fusion.refs_6_.refs_5_), custom_call_target="tpu_custom_call" | custom-call | tf_op jit(solution)/shard_map/operator_next/pallas_call | solution.py:473
  209.7 0.0 copy-done.1
  209.7 0.0 copy-start.4
  209.7 1.1 copy-done.4
  210.8 0.0 copy-start.7
  210.8 0.9 copy-done.7
  211.7 0.0 copy-start.9
  211.7 0.9 copy-done.9
  212.6 9.7 %ritz_last.1 = (f32[1024,64]{1,0:T(8,128)S(1)}, f32[1024,64]{1,0:T(8,128)S(1)}, f32[1024,64]{1,0:T(8,128)S(1)}) custom-call(f32[8,32,128]{2,1,0:T(8,128)S(1)} %copy-done.9, f32[192,192]{1,0:T(8,128)S(1)} %copy-done.7, f32[192,1024]{1,0:T(8,128)S(1)} %copy-done.1, f32[192,1024]{1,0:T(8,128)S(1)} %copy-done.4), custom_call_target="tpu_custom_call" | custom-call | tf_op jit(solution)/shard_map/ritz_last/pallas_call | solution.py:550
  222.4 0.9 copy.20
  223.3 0.9 copy.21
  224.2 0.9 copy.22
  (2 shorter events, 0.0 us)
Async XLA Ops:
  119.4 1.1 copy-start.2
  120.5 1.1 copy-start.3
  121.6 0.9 copy-start.6
  122.6 0.9 copy-start.8
  133.0 0.9 copy-start
  133.9 0.8 copy-start.5
  134.7 74.9 %copy-start.1 = (f32[192,1024]{1,0:T(8,128)S(1)}, f32[192,1024]{1,0:T(8,128)}, u32[]{:S(2)}) copy-start(f32[192,1024]{1,0:T(8,128)} %copy-done) | copy-start | bytes 2359300
  209.7 1.1 copy-start.4
  210.8 0.9 copy-start.7
  211.7 0.9 copy-start.9

commit v2 on v0

v2 whole, which is shorter than its diff:
```python
import functools

import jax
import jax.numpy as jnp
from jax import lax
from jax.experimental import pallas as pl
from jax.experimental.pallas import tpu as pltpu
from jax.sharding import PartitionSpec as P

RR_STEPS = 3
K = 64
W3 = 3 * K
TILE = 128
BLOCKS = 8
SLOTS = 64
ROWS = 16
COLS = 8
SIDE = 4
NODES = BLOCKS * TILE
NODE_TOTAL = NODES * ROWS * COLS
F32 = jnp.float32
BF16 = jnp.bfloat16
MESH = pl.DeviceIdType.MESH
STEP = 8
HALF = BLOCKS // 2


def dot_nn(a, b):
    return lax.dot_general(
        a, b, (((1,), (0,)), ((), ())), precision=lax.Precision.HIGHEST, preferred_element_type=F32
    )


def dot_nt(a, b):
    return lax.dot_general(
        a, b, (((1,), (1,)), ((), ())), precision=lax.Precision.HIGHEST, preferred_element_type=F32
    )


def dot_tn(a, b):
    return lax.dot_general(
        a, b, (((0,), (0,)), ((), ())), precision=lax.Precision.HIGHEST, preferred_element_type=F32
    )


def eye(n):
    return jnp.where(
        lax.broadcasted_iota(jnp.int32, (n, n), 0) == lax.broadcasted_iota(jnp.int32, (n, n), 1), 1.0, 0.0
    ).astype(F32)


def inverse_factor(a):
    n = K
    both = jnp.concatenate([a, eye(n)], axis=1)
    tiles = [both[8 * t : 8 * t + 8, :] for t in range(n // 8)]
    shape = (8, 2 * n)
    sub = lax.broadcasted_iota(jnp.int32, shape, 0)
    done = []

    def lanes(v, k):
        return jnp.broadcast_to(v[:, k : k + 1], shape)

    for k in range(0, n, STEP):
        t0 = k // STEP
        r = [jnp.broadcast_to(tiles[t0][i : i + 1, :], shape) for i in range(STEP)]
        p = {(i, j): lanes(r[i], k + j) for i in range(STEP) for j in range(i, STEP)}
        pulled, gains = {}, {}
        row = None
        for i in range(0, STEP, 2):
            j = i + 1
            a_, b_, c_ = p[i, i], p[i, j], p[j, j]
            inverse = 1.0 / (a_ * c_ - b_ * b_)
            ia, ib, ic = a_ * inverse, b_ * inverse, c_ * inverse
            pulled[i], pulled[j] = ic * r[i] - ib * r[j], ia * r[j] - ib * r[i]
            for m in range(j + 1, STEP):
                gains[i, m] = ic * p[i, m] - ib * p[j, m]
                gains[j, m] = ia * p[j, m] - ib * p[i, m]
            for m in range(j + 1, STEP):
                r[m] = r[m] - (p[i, m] * pulled[i] + p[j, m] * pulled[j])
                for l in range(m, STEP):
                    p[m, l] = p[m, l] - (p[i, m] * gains[i, l] + p[j, m] * gains[j, l])
            slope = b_ / a_
            top = r[i] * lax.rsqrt(a_)
            low = (r[j] - slope * r[i]) * lax.rsqrt(c_ - slope * b_)
            row = top if row is None else jnp.where(sub == i, top, row)
            row = jnp.where(sub == j, low, row)
        done.append(row)
        for t in range(t0 + 1, n // 8):
            c = [lanes(tiles[t], k + j) for j in range(STEP)]
            change = None
            for i in range(0, STEP, 2):
                j = i + 1
                part = c[i] * pulled[i] + c[j] * pulled[j]
                change = part if change is None else change + part
                for m in range(j + 1, STEP):
                    c[m] = c[m] - (c[i] * gains[i, m] + c[j] * gains[j, m])
            tiles[t] = tiles[t] - change
    return jnp.concatenate(done, axis=0)[:, n:]


class Here:
    def __init__(self):
        self.row, self.col = lax.axis_index("row"), lax.axis_index("col")
        self.x, self.y = self.row // SIDE, lax.rem(self.row, SIDE)
        self.z, self.core = self.col // 2, lax.rem(self.col, 2)

    def at(self, axis, step):
        return lax.rem((self.x, self.y)[axis] + step + SIDE, SIDE)

    def beside(self, axis, step):
        if axis == 0:
            return (self.at(0, step) * SIDE + self.y, self.col)
        return (self.x * SIDE + self.at(1, step), self.col)

    def level(self, step):
        return lax.rem(self.z + step + SIDE, SIDE) * 2 + self.core

    def send(self, src, dst, send_sem, recv_sem, where):
        copy = pltpu.make_async_remote_copy(
            src_ref=src, dst_ref=dst, send_sem=send_sem, recv_sem=recv_sem, device_id=where, device_id_type=MESH
        )
        copy.start()
        return copy


def wait_for(ref, sem):
    pltpu.make_async_copy(ref, ref, sem).wait()


class Reduce:
    def __init__(self, here, part, spread, cross, out, sent, came):
        self.here, self.part, self.spread, self.cross, self.out = here, part, spread, cross, out
        self.sent, self.came = sent, came

    def pack(self, full):
        for c in range(W3 // 16):
            self.part[c] = full[16 * c : 16 * c + 16, 0:TILE]
        for c in range(K // 16):
            self.part[12 + c] = jnp.zeros((16, TILE), F32)
            self.part[12 + c, :, 0:K] = full[2 * K + 16 * c : 2 * K + 16 * c + 16, TILE : TILE + K]

    def start(self):
        h = self.here
        self.spread[h.row] = self.part[h.row]
        for o in range(1, ROWS):
            to = lax.rem(h.row + o, ROWS)
            h.send(self.part.at[to], self.spread.at[h.row], self.sent.at[0], self.came.at[0], (to, h.col))

    def over_col(self):
        h = self.here
        wait_for(self.spread.at[pl.ds(0, ROWS - 1)], self.came.at[0])
        total = self.spread[0]
        for c in range(1, ROWS):
            total = total + self.spread[c]
        self.cross[h.col] = total
        for o in range(1, COLS):
            to = lax.rem(h.col + o, COLS)
            h.send(self.cross.at[h.col], self.cross.at[h.col], self.sent.at[1], self.came.at[1], (h.row, to))

    def share(self):
        h = self.here
        wait_for(self.cross.at[pl.ds(0, COLS - 1)], self.came.at[1])
        total = self.cross[0]
        for c in range(1, COLS):
            total = total + self.cross[c]
        self.out[h.row] = total
        for o in range(1, ROWS):
            to = lax.rem(h.row + o, ROWS)
            h.send(self.out.at[h.row], self.out.at[h.row], self.sent.at[2], self.came.at[2], (to, h.col))

    def finish(self):
        wait_for(self.out.at[pl.ds(0, ROWS - 1)], self.came.at[2])

    def close(self):
        wait_for(self.part.at[pl.ds(0, ROWS - 1)], self.sent.at[0])
        wait_for(self.cross.at[pl.ds(0, COLS - 1)], self.sent.at[1])
        wait_for(self.out.at[pl.ds(0, ROWS - 1)], self.sent.at[2])


def symmetric(cross):
    return 0.5 * (cross + jnp.transpose(cross))


class Group:
    def __init__(self, here, width, extra, unroll, refs):
        self.here, self.width, self.extra, self.unroll = here, width, extra, unroll
        self.quarter = width // 4
        (
            self.v, self.acc, self.sb, self.f1, self.n1, self.c1, self.tb, self.last, self.sent, self.came
        ) = refs

    def prepare(self, st, base, scale):
        col = self.here.col
        for b in range(BLOCKS):
            d_b = scale[b : b + 1, :]
            block = st[base : base + self.width, b * TILE : (b + 1) * TILE] * d_b
            self.v[col, b, 0 : self.width, :] = block.astype(BF16)
            if self.extra:
                sub = lax.broadcasted_iota(jnp.int32, (16, TILE), 0)
                self.v[col, b, self.width : self.width + 16, :] = jnp.where(sub == 0, d_b, 0.0).astype(BF16)

    def pass_on(self, n, src, where):
        self.here.send(src, src, self.sent.at[0], self.came.at[n], where)

    def gather_start(self):
        h = self.here
        self.up, self.down = (h.row, h.level(1)), (h.row, h.level(-1))
        self.mate = (h.row, h.z * 2 + 1 - h.core)
        mine = self.v.at[h.col]
        self.pass_on(0, mine, self.up)
        self.pass_on(1, mine, self.down)
        self.pass_on(4, mine, self.mate)

    def gather_near(self):
        h = self.here
        wait_for(self.v.at[0], self.came.at[0])
        self.pass_on(2, self.v.at[h.level(-1), pl.ds(0, HALF)], self.up)
        self.pass_on(4, self.v.at[h.level(-1)], self.mate)
        wait_for(self.v.at[0], self.came.at[1])
        self.pass_on(3, self.v.at[h.level(1), pl.ds(HALF, HALF)], self.down)
        self.pass_on(4, self.v.at[h.level(1)], self.mate)

    def gather_far(self):
        h = self.here
        wait_for(self.v.at[0, pl.ds(0, HALF)], self.came.at[2])
        self.pass_on(4, self.v.at[h.level(2), pl.ds(0, HALF)], self.mate)
        wait_for(self.v.at[0, pl.ds(0, HALF)], self.came.at[3])
        self.pass_on(4, self.v.at[h.level(2), pl.ds(HALF, HALF)], self.mate)

    def gather_finish(self):
        wait_for(self.v.at[pl.ds(0, SIDE)], self.came.at[4])

    def near_total(self):
        h = self.here
        ones = jnp.ones((TILE, TILE), BF16)
        total = jnp.zeros((self.width + self.extra, TILE), F32)
        for j in (h.col, h.level(-1), h.level(1)):
            for b in range(BLOCKS):
                total = total + lax.dot_general(
                    self.v[j, b], ones, (((1,), (1,)), ((), ())), preferred_element_type=F32
                )
        return total

    def products(self, tiles, col_ref, link, start=0, stop=SLOTS):
        if start == 0:
            self.acc[SLOTS] = jnp.zeros((self.width + self.extra, TILE), F32)

        def step(t, carry):
            found = []
            for u in range(self.unroll):
                s = self.unroll * t + u
                c = col_ref[0, s]
                found.append(
                    lax.dot_general(
                        self.v[c // BLOCKS, lax.rem(c, BLOCKS)],
                        tiles[s],
                        (((1,), (1,)), ((), ())),
                        preferred_element_type=F32,
                    )
                )
            for u in range(self.unroll):
                s = self.unroll * t + u
                self.acc[s] = found[u] + self.acc[link[1, s]]
            return carry

        lax.fori_loop(start // self.unroll, stop // self.unroll, step, 0)

    def place(self, link, mean=None, weights=None):
        h, quarter = self.here, self.quarter

        def blocks_of(dx, dy):
            to = dx * SIDE + dy
            for b in range(BLOCKS):
                block = self.acc[link[0, to * BLOCKS + b]]
                if self.extra:
                    weight = block[self.width : self.width + 1, :]
                    weights[to, b : b + 1, :] = weight
                    block = block[0 : self.width, :]
                elif mean is not None:
                    weight = weights[to, b : b + 1, :]
                if mean is not None:
                    block = block - mean * weight
                block = block.astype(BF16)
                for q in range(4):
                    piece = block[q * quarter : (q + 1) * quarter, :]
                    if q < 2:
                        self.sb[q, dx, dy, b] = piece
                    else:
                        self.sb[q, dy, dx, b] = piece

        def far_x(t, carry):
            blocks_of(h.at(0, 2), t)
            return carry

        def far_y(t, carry):
            blocks_of(h.at(0, 3 + t), h.at(1, 2))
            return carry

        def others(t, carry):
            blocks_of(h.at(0, 3 + t // 3), h.at(1, 3 + lax.rem(t, 3)))
            return carry

        lax.fori_loop(0, SIDE, far_x, 0)
        self.far(0)
        lax.fori_loop(0, 3, far_y, 0)
        self.far(2)
        lax.fori_loop(0, 9, others, 0)
        self.near()

    def far(self, first):
        h = self.here
        for q in (first, first + 1):
            axis, sign = q // 2, 1 - 2 * (q % 2)
            h.send(self.sb.at[q, h.at(axis, 2)], self.f1.at[q], self.sent.at[1], self.came.at[5 + q], h.beside(axis, sign))

    def near(self):
        h = self.here
        for q in range(4):
            axis, sign = q // 2, 1 - 2 * (q % 2)
            h.send(self.sb.at[q, h.at(axis, -sign)], self.n1.at[q], self.sent.at[1], self.came.at[9 + q], h.beside(axis, -sign))

    def meet(self):
        h = self.here
        for q in range(4):
            axis, sign = q // 2, 1 - 2 * (q % 2)
            wait_for(self.f1.at[q], self.came.at[5 + q])
            to = h.at(axis, sign)

            def step(d, carry, q=q, to=to):
                total = self.sb[q, to, d].astype(F32) + self.f1[q, d].astype(F32)
                self.sb[q, to, d] = total.astype(BF16)
                return carry

            lax.fori_loop(0, SIDE, step, 0)
            h.send(self.sb.at[q, to], self.c1.at[q], self.sent.at[1], self.came.at[9 + q], h.beside(axis, sign))

    def turn(self):
        h = self.here
        for q in range(4):
            axis = q // 2
            wait_for(self.sb.at[q, pl.ds(0, 2)], self.came.at[9 + q])
            me = h.at(axis, 0)

            def step(d, carry, q=q, me=me):
                total = self.sb[q, me, d].astype(F32) + self.n1[q, d].astype(F32) + self.c1[q, d].astype(F32)
                self.tb[q, d] = total.astype(BF16)
                return carry

            lax.fori_loop(0, SIDE, step, 0)
            for o in (2, 1, 3):
                h.send(
                    self.tb.at[q, h.at(1 - axis, o)], self.last.at[q, o - 1], self.sent.at[2], self.came.at[13 + q],
                    h.beside(1 - axis, o),
                )

    def finish(self, out, base, scale, back=None):
        h, quarter = self.here, self.quarter
        for q in range(4):
            me = h.at(1 - q // 2, 0)
            wait_for(self.last.at[q], self.came.at[13 + q])
            first = base + q * quarter
            for b in range(BLOCKS):
                lanes = slice(b * TILE, (b + 1) * TILE)
                total = self.tb[q, me, b].astype(F32)
                for o in range(SIDE - 1):
                    total = total + self.last[q, o, b].astype(F32)
                if back is not None:
                    total = total + back[first : first + quarter, lanes]
                out[first : first + quarter, lanes] = total * scale[b : b + 1, :]

    def close(self):
        wait_for(self.v.at[pl.ds(0, COLS - 1)], self.sent.at[0])
        wait_for(self.sb.at[pl.ds(0, 3)], self.sent.at[1])
        wait_for(self.tb.at[pl.ds(0, 3)], self.sent.at[2])


class Factor:
    def __init__(self, sums, out):
        self.sums, self.out = sums, out

    def gram(self, r, c):
        if (r, c) == (2, 2):
            pieces = [self.sums[12 + i, :, 0:K] for i in range(4)]
        else:
            pieces = [self.sums[4 * r + i, :, c * K : c * K + K] for i in range(4)]
        return jnp.concatenate(pieces, axis=0) * (1.0 / NODE_TOTAL)

    def first(self):
        self.k11 = inverse_factor(self.gram(0, 0))
        self.l21 = dot_nt(self.gram(1, 0), self.k11)
        self.l31 = dot_nt(self.gram(2, 0), self.k11)
        self.s22 = self.gram(1, 1) - dot_nt(self.l21, self.l21)

    def second(self):
        self.k22 = inverse_factor(self.s22)
        self.l32 = dot_nt(self.gram(2, 1) - dot_nt(self.l31, self.l21), self.k22)
        self.s33 = self.gram(2, 2) - dot_nt(self.l31, self.l31) - dot_nt(self.l32, self.l32)

    def third(self):
        k33 = inverse_factor(self.s33)
        k21 = -dot_nn(self.k22, dot_nn(self.l21, self.k11))
        k32 = -dot_nn(k33, dot_nn(self.l32, self.k22))
        k31 = -dot_nn(k33, dot_nn(self.l31, self.k11) + dot_nn(self.l32, k21))
        self.out[...] = jnp.zeros((W3, W3), F32)
        for (r, c), block in {
            (0, 0): self.k11, (1, 0): k21, (1, 1): self.k22, (2, 0): k31, (2, 1): k32, (2, 2): k33
        }.items():
            self.out[r * K : r * K + K, c * K : c * K + K] = block


def full_symmetric(sums):
    left = jnp.concatenate([sums[c] for c in range(12)], axis=0)
    corner = jnp.concatenate([sums[12 + c, :, 0:K] for c in range(4)], axis=0)
    right = jnp.concatenate([jnp.transpose(left[TILE:W3, :]), corner], axis=0)
    return jnp.concatenate([left, right], axis=1) * (1.0 / NODE_TOTAL)


def ritz(sums, kinv):
    reduced = symmetric(dot_nt(dot_nn(kinv, full_symmetric(sums)), kinv))
    shifted = reduced + 4.0 * eye(W3)
    moved = shifted[0:K, :]
    for inner in range(RR_STEPS - 1):
        factor = inverse_factor(dot_nt(moved, moved))
        moved = dot_nn(factor, dot_nn(moved, shifted))
    factor = inverse_factor(dot_nt(moved, moved))
    theta = dot_nt(dot_nn(factor, dot_nt(dot_nn(moved, reduced), moved)), factor)
    c_t = dot_nn(factor, dot_nn(moved, kinv))
    return c_t, dot_tn(theta, c_t)


def whole_kernel(*refs):
    x_hbm, r_hbm, p_hbm, tiles_hbm = refs[:4]
    small_hbm = refs[4:8]
    h_out, kinv, st_out, ast_out = refs[8:12]
    st, ast, st2, ast2, tiles, link_v, link, weights, others = refs[12:21]
    nc_ref, row_ref, col_ref, count_ref = refs[21:25]
    load_sems, small_sems, link_sem, m_s, m_r = refs[25:30]
    rest = refs[30:]
    here = Here()
    reduces, groups = [], []
    for n in range(4):
        reduces.append(Reduce(here, *rest[:6]))
        rest = rest[6:]
    for width, extra, unroll in ((K, 16, 8), (2 * K, 0, 4), (K, 0, 8)):
        groups.append(Group(here, width, extra, unroll, rest[:10]))
        rest = rest[10:]
    sum_g, sum_h, sum_g2, sum_h2 = reduces
    thin, wide, again = groups
    row, col = here.row, here.col

    barrier = pltpu.get_barrier_semaphore()
    for o in range(1, ROWS):
        pl.semaphore_signal(barrier, inc=1, device_id=(lax.rem(row + o, ROWS), col), device_id_type=MESH)
    for o in range(1, COLS):
        pl.semaphore_signal(barrier, inc=1, device_id=(row, lax.rem(col + o, COLS)), device_id_type=MESH)
    loads = [
        pltpu.make_async_copy(p_hbm, st.at[pl.ds(2 * K, K)], load_sems.at[0]),
        pltpu.make_async_copy(x_hbm, st.at[pl.ds(0, K)], load_sems.at[1]),
        pltpu.make_async_copy(r_hbm, st.at[pl.ds(K, K)], load_sems.at[2]),
        pltpu.make_async_copy(tiles_hbm, tiles, load_sems.at[3]),
    ]
    small = [
        pltpu.make_async_copy(src, dst, small_sems.at[n])
        for n, (src, dst) in enumerate(zip(small_hbm, (nc_ref, row_ref, col_ref, count_ref)))
    ]
    for load in small + loads:
        load.start()
    for load in small:
        load.wait()

    along = lax.broadcasted_iota(jnp.int32, (SLOTS, SLOTS), 1)
    slot = lax.broadcasted_iota(jnp.int32, (SLOTS, SLOTS), 0)
    targets = jnp.broadcast_to(row_ref[...], (SLOTS, SLOTS))
    target = jnp.sum(jnp.where(slot == along, targets, 0), axis=1, keepdims=True)
    live = count_ref[0, 0]
    before = jnp.where((target == targets) & (slot < along) & (slot < live), slot, -1)
    before = jnp.max(before, axis=0, keepdims=True)
    slot = lax.broadcasted_iota(jnp.int32, (SLOTS, TILE), 0)
    final = jnp.where((target == lax.broadcasted_iota(jnp.int32, (SLOTS, TILE), 1)) & (slot < live), slot, -1)
    final = jnp.max(final, axis=0, keepdims=True)
    link_v[...] = jnp.full((8, TILE), SLOTS, jnp.int32)
    link_v[0:1, :] = jnp.where(final < 0, SLOTS, final)
    link_v[1:2, 0:SLOTS] = jnp.where(before < 0, SLOTS, before)
    link_copy = pltpu.make_async_copy(link_v, link, link_sem)
    link_copy.start()

    scale = 1.0 / jnp.sqrt(nc_ref[...].astype(F32))
    loads[0].wait()
    thin.prepare(st, 2 * K, scale)
    pl.semaphore_wait(barrier, ROWS - 1 + COLS - 1)

    thin.gather_start()
    loads[1].wait()
    loads[2].wait()
    wide.prepare(st, 0, scale)
    stv = st[...]
    sum_g.pack(dot_nt(stv, stv))
    sum_g.start()
    thin.gather_near()
    wide.gather_start()
    thin_total = thin.near_total()
    nodes = thin_total[K : K + 1, :]
    thin_mean = thin_total[0:K, :] / nodes
    sum_g.over_col()
    thin.gather_far()
    loads[3].wait()
    link_copy.wait()
    thin.gather_finish()
    thin.products(tiles, col_ref, link)
    wide.gather_near()
    thin.place(link, thin_mean, weights)
    wide.gather_far()
    sum_g.share()
    wide_mean = wide.near_total() / nodes
    weight_rows = [
        jnp.transpose(wide_mean)[0:1, :],
        jnp.transpose(jnp.concatenate([thin_mean, jnp.zeros((K, TILE), F32)], axis=0))[0:1, :],
    ]
    for i in range(ROWS):
        weights[i, 8:9, :] = weight_rows[0]
        weights[i, 9:10, :] = weight_rows[1]
        weights[i, 10:16, :] = jnp.zeros((6, TILE), F32)
    others[row] = weights[row]
    for o in range(1, ROWS):
        to = lax.rem(row + o, ROWS)
        here.send(weights.at[to], others.at[row], m_s, m_r, (to, col))
    wide.gather_finish()
    wide.products(tiles, col_ref, link, 0, SLOTS // 2)
    thin.meet()
    wide.products(tiles, col_ref, link, SLOTS // 2, SLOTS)
    wide.place(link, wide_mean, weights)
    sum_g.finish()
    factor = Factor(sum_g.out, kinv)
    factor.first()
    thin.turn()
    factor.second()
    wide.meet()
    factor.third()
    wait_for(others.at[pl.ds(0, ROWS - 1)], m_r)
    means = jnp.concatenate([others[:, 8, :], others[:, 9, :]], axis=1)
    back = dot_tn(means, jnp.concatenate([others[:, b, :] for b in range(BLOCKS)], axis=1))
    thin.finish(ast, 2 * K, scale, back)
    wide.turn()
    wide.finish(ast, 0, scale, back)
    astv = ast[...]
    sum_h.pack(symmetric(dot_nt(stv, astv)))
    sum_h.start()
    sum_h.over_col()
    sum_h.share()
    sum_h.finish()

    c_t, drop_t = ritz(sum_h.out, kinv[...])
    st2[K : 2 * K, :] = dot_nn(c_t, astv) - dot_nn(drop_t, stv)
    again.prepare(st2, K, scale)
    again.gather_start()
    cp_t = jnp.where(lax.broadcasted_iota(jnp.int32, (K, W3), 1) < K, 0.0, c_t)
    both = jnp.concatenate([c_t, cp_t], axis=0)
    moved = dot_nn(both, stv)
    st2[0:K, :] = moved[0:K, :]
    st2[2 * K : W3, :] = moved[K : 2 * K, :]
    stv2 = st2[...]
    sum_g2.pack(dot_nt(stv2, stv2))
    sum_g2.start()
    image = dot_nn(both, astv)
    ast2[0:K, :] = image[0:K, :]
    ast2[2 * K : W3, :] = image[K : 2 * K, :]
    again.gather_near()
    sum_g2.over_col()
    again.gather_far()
    again.gather_finish()
    again.products(tiles, col_ref, link)
    sum_g2.share()
    again.place(link)
    sum_g2.finish()
    again.meet()
    factor = Factor(sum_g2.out, kinv)
    factor.first()
    factor.second()
    again.turn()
    factor.third()
    again.finish(ast2, K, scale)
    astv2 = ast2[...]
    stores = [pltpu.make_async_copy(st2, st_out, load_sems.at[0]), pltpu.make_async_copy(ast2, ast_out, load_sems.at[1])]
    for store in stores:
        store.start()
    sum_h2.pack(symmetric(dot_nt(stv2, astv2)))
    sum_h2.start()
    sum_h2.over_col()
    sum_h2.share()
    sum_h2.finish()

    h_out[...] = sum_h2.out[...]
    for store in stores:
        store.wait()
    wait_for(weights.at[pl.ds(0, ROWS - 1)], m_s)
    for each in reduces + groups:
        each.close()


def whole_call(x_t, r_t, p_t, tiles, counts, tile_row, tile_col, tile_count):
    vmem = pl.BlockSpec(memory_space=pltpu.VMEM)
    hbm = pl.BlockSpec(memory_space=pltpu.HBM)
    dma = pltpu.SemaphoreType.DMA
    scratch = [
        pltpu.VMEM((W3, NODES), F32),
        pltpu.VMEM((W3, NODES), F32),
        pltpu.VMEM((W3, NODES), F32),
        pltpu.VMEM((W3, NODES), F32),
        pltpu.VMEM((SLOTS, TILE, TILE), BF16),
        pltpu.VMEM((8, TILE), jnp.int32),
        pltpu.SMEM((8, TILE), jnp.int32),
        pltpu.VMEM((ROWS, 16, TILE), F32),
        pltpu.VMEM((ROWS, 16, TILE), F32),
        pltpu.VMEM((BLOCKS, TILE), jnp.int32),
        pltpu.VMEM((1, SLOTS), jnp.int32),
        pltpu.SMEM((1, SLOTS), jnp.int32),
        pltpu.SMEM((1, 1), jnp.int32),
        dma((4,)),
        dma((4,)),
        dma(()),
        dma(()),
        dma(()),
    ]
    for n in range(4):
        scratch += [
            pltpu.VMEM((ROWS, 16, TILE), F32),
            pltpu.VMEM((ROWS, 16, TILE), F32),
            pltpu.VMEM((COLS, 16, TILE), F32),
            pltpu.VMEM((ROWS, 16, TILE), F32),
            dma((3,)),
            dma((3,)),
        ]
    for width, extra in ((K, 16), (2 * K, 0), (K, 0)):
        quarter = width // 4
        scratch += [
            pltpu.VMEM((COLS, BLOCKS, width + extra, TILE), BF16),
            pltpu.VMEM((SLOTS + 1, width + extra, TILE), F32),
            pltpu.VMEM((4, SIDE, SIDE, BLOCKS, quarter, TILE), BF16),
        ]
        scratch += [pltpu.VMEM((4, SIDE, BLOCKS, quarter, TILE), BF16)] * 4
        scratch += [pltpu.VMEM((4, SIDE - 1, BLOCKS, quarter, TILE), BF16)]
        scratch += [dma((3,)), dma((17,))]
    return pl.pallas_call(
        whole_kernel,
        name="iterations",
        out_shape=[
            jax.ShapeDtypeStruct((ROWS, 16, TILE), F32),
            jax.ShapeDtypeStruct((W3, W3), F32),
            jax.ShapeDtypeStruct((W3, NODES), F32),
            jax.ShapeDtypeStruct((W3, NODES), F32),
        ],
        in_specs=[hbm] * 8,
        out_specs=[vmem, vmem, hbm, hbm],
        scratch_shapes=scratch,
        compiler_params=pltpu.CompilerParams(
            collective_id=0, has_side_effects=True, vmem_limit_bytes=60 << 20
        ),
    )(x_t, r_t, p_t, tiles, counts, tile_row, tile_col, tile_count)


def last_kernel(sums, kinv, st_hbm, ast_hbm, x_out, r_out, p_out, st, ast, sems):
    loads = [pltpu.make_async_copy(st_hbm, st, sems.at[0]), pltpu.make_async_copy(ast_hbm, ast, sems.at[1])]
    for load in loads:
        load.start()
    c_t, drop_t = ritz(sums, kinv[...])
    for load in loads:
        load.wait()
    cp_t = jnp.where(lax.broadcasted_iota(jnp.int32, (K, W3), 1) < K, 0.0, c_t)
    moved = dot_nn(jnp.concatenate([c_t, cp_t, drop_t], axis=0), st[...])
    x_out[...] = moved[0:K, :]
    p_out[...] = moved[K : 2 * K, :]
    r_out[...] = dot_nn(c_t, ast[...]) - moved[2 * K : W3, :]


def last_call(sums, kinv, st, ast):
    vmem = pl.BlockSpec(memory_space=pltpu.VMEM)
    hbm = pl.BlockSpec(memory_space=pltpu.HBM)
    return pl.pallas_call(
        last_kernel,
        name="last_update",
        out_shape=[jax.ShapeDtypeStruct((K, NODES), F32)] * 3,
        in_specs=[vmem, vmem, hbm, hbm],
        out_specs=[vmem] * 3,
        scratch_shapes=[
            pltpu.VMEM((W3, NODES), F32), pltpu.VMEM((W3, NODES), F32), pltpu.SemaphoreType.DMA((2,))
        ],
        compiler_params=pltpu.CompilerParams(vmem_limit_bytes=60 << 20),
    )(sums, kinv, st, ast)


def per_device(
    x_block, r_block, p_block, neighbor_count, tile_values, tile_row, tile_col, tile_count
):
    whole = whole_call(
        x_block.T,
        r_block.T,
        p_block.T,
        tile_values[0, 0],
        neighbor_count.reshape(BLOCKS, TILE),
        tile_row[0],
        tile_col[0],
        tile_count,
    )

    x_t, r_t, p_t = last_call(*whole)
    return x_t.T, r_t.T, p_t.T


def solution(mesh):
    placed = (
        P(("col", "row"), None),
        P(("col", "row"), None),
        P(("col", "row"), None),
        P(("col", "row")),
        P("row", "col", None, None, None),
        P("row", "col", None),
        P("row", "col", None),
        P("row", "col"),
    )
    return jax.shard_map(
        per_device,
        mesh=mesh,
        in_specs=placed,
        out_specs=(P(("col", "row"), None), P(("col", "row"), None), P(("col", "row"), None)),
        check_vma=False,
    )
```

time: 861 us -> 148 us (0.17)
  waiting for transfers between devices: 534 us -> 0 us
  other arithmetic: 210 us -> 0 us
  Pallas kernels: 0 us -> 147 us
  local copies, waits for them, and re-layouts: 52.8 us -> 0 us
  matrix products: 38.8 us -> 0 us
  between operations: 18.5 us -> 1.47 us
    psum x2 -> x0, waiting for transfers between devices: 292 us -> none  [per_device(): lax.psum((small_product(block_panel.T, block_panel), small_product(block_...]
    reduce_scatter x2 -> x0, waiting for transfers between devices: 184 us -> none  [per_device(): lax.psum_scatter(partial_value, 'row', scatter_dimension=0, tiled=True)]
    another operation x56 -> x0, other arithmetic: 170 us -> none  [the longest x14 57.4 us: ritz_step(): lower = jnp.linalg.cholesky(gram_g)]
    pallas_call x0 -> x2, Pallas kernels: none -> 147 us  [the longest x1 135 us: whole_call(): pl.pallas_call(whole_kernel, name='iterations', out_shape=[jax.ShapeDtype...]
    all_gather x2 -> x0, waiting for transfers between devices: 57.9 us -> none  [per_device(): gathered = lax.all_gather(scaled, 'col', axis=0, tiled=True)]
    scatter-add x2 -> x0, other arithmetic: 33.2 us -> none  [per_device(): jax.ops.segment_sum(tile_contributions, targets, num_segments=row_process...]
    dot_general x30 -> x0, matrix products: 31.2 us -> none  [the longest x28 18.5 us: small_product(): return jnp.matmul(left, right, precision=lax.Precision.HIGHEST)]
    reshape x4 -> x0, local copies, waits for them, and re-layouts: 28.2 us -> none  [the longest x2 21 us: per_device(): partial_value.reshape(row_processors * row_count, panel_width)]
  transfers between devices with their start and end apart: 6 -> 0, of which waited for: 6 -> 0; matrix products, arithmetic and copies ran while one was open for 0% -> 0% of each run, Pallas kernels for 0% -> 0%
where the time goes in v2:
time: 148 us
  Pallas kernels  147 us (99%)
    pallas_call x1, Pallas kernels, whole_call(): pl.pallas_call(whole_kernel, name='iterations', out_shape=[jax.ShapeDtype...  135 us
    pallas_call x1, Pallas kernels, last_call(): pl.pallas_call(last_kernel, name='last_update', out_shape=[jax.ShapeDtype...  12.2 us

profile of v2, /device:TPU:1, one launch (start us, length us, event | category | flops | bytes accessed | tf_op | source)
XLA Modules:
  0.0 148.2 jit_solution(3614737990465429225)
XLA Ops:
  1.3 134.6 %iterations.1 = (f32[16,16,128]{2,1,0:T(8,128)}, f32[192,192]{1,0:T(8,128)}, f32[192,1024]{1,0:T(8,128)}, f32[192,1024]{1,0:T(8,128)}) custom-call(f32[64,1024]{1,0:T(8,128)} %bitcast.11, f32[64,1024]{1,0:T(8,128)} %bitcast.12, f32[64,1024]{1,0:T(8,128)} %bitcast.13, bf16[64,128,128]{2,1,0:T(8,128)(2,1)} %bitcast.10, s32[8,128]{1,0:T(8,128)} %bitcast.14, ...), custom_call_target="tpu_custom_call" | custom-call | tf_op jit(solution)/shard_map/iterations/pallas_call | solution.py:643
  135.9 12.2 %last_update.1 = (f32[64,1024]{1,0:T(8,128)}, f32[64,1024]{1,0:T(8,128)}, f32[64,1024]{1,0:T(8,128)}) custom-call(f32[16,16,128]{2,1,0:T(8,128)} %get-tuple-element.10.sums, f32[192,192]{1,0:T(8,128)} %get-tuple-element.11.kinv, f32[192,1024]{1,0:T(8,128)} %get-tuple-element.12.st_hbm, f32[192,1024]{1,0:T(8,128)} %get-tuple-element.13.ast_hbm), custom_call_target="tpu_custom_call" | custom-call | tf_op jit(solution)/shard_map/last_update/pallas_call | solution.py:678

commit v3 on v2

--- a/solution.py
+++ b/solution.py
@@ -63,7 +63,8 @@
     for k in range(0, n, STEP):
         t0 = k // STEP
         r = [jnp.broadcast_to(tiles[t0][i : i + 1, :], shape) for i in range(STEP)]
-        p = {(i, j): lanes(r[i], k + j) for i in range(STEP) for j in range(i, STEP)}
+        own = [lanes(tiles[t0], k + j) for j in range(STEP)]
+        p = {(i, j): jnp.broadcast_to(own[j][i : i + 1, :], shape) for i in range(STEP) for j in range(i, STEP)}
         pulled, gains = {}, {}
         row = None
         for i in range(0, STEP, 2):
@@ -128,8 +129,8 @@
 
 
 class Reduce:
-    def __init__(self, here, part, spread, cross, out, sent, came):
-        self.here, self.part, self.spread, self.cross, self.out = here, part, spread, cross, out
+    def __init__(self, here, part, spread, cross, pair, out, sent, came):
+        self.here, self.part, self.spread, self.cross, self.pair, self.out = here, part, spread, cross, pair, out
         self.sent, self.came = sent, came
 
     def pack(self, full):
@@ -146,24 +147,27 @@
             to = lax.rem(h.row + o, ROWS)
             h.send(self.part.at[to], self.spread.at[h.row], self.sent.at[0], self.came.at[0], (to, h.col))
 
-    def over_col(self):
+    def over_z(self):
         h = self.here
         wait_for(self.spread.at[pl.ds(0, ROWS - 1)], self.came.at[0])
         total = self.spread[0]
         for c in range(1, ROWS):
             total = total + self.spread[c]
-        self.cross[h.col] = total
-        for o in range(1, COLS):
-            to = lax.rem(h.col + o, COLS)
-            h.send(self.cross.at[h.col], self.cross.at[h.col], self.sent.at[1], self.came.at[1], (h.row, to))
+        self.cross[h.z] = total
+        for o in range(1, SIDE):
+            h.send(self.cross.at[h.z], self.cross.at[h.z], self.sent.at[1], self.came.at[1], (h.row, h.level(o)))
+
+    def over_core(self):
+        h = self.here
+        wait_for(self.cross.at[pl.ds(0, SIDE - 1)], self.came.at[1])
+        self.pair[h.core] = (self.cross[0] + self.cross[1]) + (self.cross[2] + self.cross[3])
+        own = self.pair.at[h.core]
+        h.send(own, own, self.sent.at[3], self.came.at[3], (h.row, h.z * 2 + 1 - h.core))
 
     def share(self):
         h = self.here
-        wait_for(self.cross.at[pl.ds(0, COLS - 1)], self.came.at[1])
-        total = self.cross[0]
-        for c in range(1, COLS):
-            total = total + self.cross[c]
-        self.out[h.row] = total
+        wait_for(self.pair.at[0], self.came.at[3])
+        self.out[h.row] = self.pair[0] + self.pair[1]
         for o in range(1, ROWS):
             to = lax.rem(h.row + o, ROWS)
             h.send(self.out.at[h.row], self.out.at[h.row], self.sent.at[2], self.came.at[2], (to, h.col))
@@ -173,7 +177,8 @@
 
     def close(self):
         wait_for(self.part.at[pl.ds(0, ROWS - 1)], self.sent.at[0])
-        wait_for(self.cross.at[pl.ds(0, COLS - 1)], self.sent.at[1])
+        wait_for(self.cross.at[pl.ds(0, SIDE - 1)], self.sent.at[1])
+        wait_for(self.pair.at[0], self.sent.at[3])
         wait_for(self.out.at[pl.ds(0, ROWS - 1)], self.sent.at[2])
 
 
@@ -210,6 +215,20 @@
         self.pass_on(0, mine, self.up)
         self.pass_on(1, mine, self.down)
         self.pass_on(4, mine, self.mate)
+
+    def gather_start_straight(self):
+        h = self.here
+        self.mate = (h.row, h.z * 2 + 1 - h.core)
+        mine = self.v.at[h.col]
+        for n, o in enumerate((1, 3, 2)):
+            self.pass_on(n, mine, (h.row, h.level(o)))
+        self.pass_on(4, mine, self.mate)
+
+    def gather_pass(self):
+        h = self.here
+        for n, o in enumerate((-1, -3, -2)):
+            wait_for(self.v.at[0], self.came.at[n])
+            self.pass_on(4, self.v.at[h.level(o)], self.mate)
 
     def gather_near(self):
         h = self.here
@@ -305,7 +324,6 @@
         lax.fori_loop(0, 3, far_y, 0)
         self.far(2)
         lax.fori_loop(0, 9, others, 0)
-        self.near()
 
     def far(self, first):
         h = self.here
@@ -439,13 +457,13 @@
     here = Here()
     reduces, groups = [], []
     for n in range(4):
-        reduces.append(Reduce(here, *rest[:6]))
-        rest = rest[6:]
-    for width, extra, unroll in ((K, 16, 8), (2 * K, 0, 4), (K, 0, 8)):
+        reduces.append(Reduce(here, *rest[:7]))
+        rest = rest[7:]
+    for width, extra, unroll in ((K, 16, 8), (K, 0, 8), (K, 0, 8), (K, 0, 8)):
         groups.append(Group(here, width, extra, unroll, rest[:10]))
         rest = rest[10:]
     sum_g, sum_h, sum_g2, sum_h2 = reduces
-    thin, wide, again = groups
+    of_p, of_r, of_x, again = groups
     row, col = here.row, here.col
 
     barrier = pltpu.get_barrier_semaphore()
@@ -486,35 +504,53 @@
 
     scale = 1.0 / jnp.sqrt(nc_ref[...].astype(F32))
     loads[0].wait()
-    thin.prepare(st, 2 * K, scale)
+    of_p.prepare(st, 2 * K, scale)
     pl.semaphore_wait(barrier, ROWS - 1 + COLS - 1)
 
-    thin.gather_start()
+    of_p.gather_start()
     loads[1].wait()
     loads[2].wait()
-    wide.prepare(st, 0, scale)
+    of_r.prepare(st, K, scale)
+    of_x.prepare(st, 0, scale)
     stv = st[...]
     sum_g.pack(dot_nt(stv, stv))
     sum_g.start()
-    thin.gather_near()
-    wide.gather_start()
-    thin_total = thin.near_total()
-    nodes = thin_total[K : K + 1, :]
-    thin_mean = thin_total[0:K, :] / nodes
-    sum_g.over_col()
-    thin.gather_far()
+    of_p.gather_near()
+    of_r.gather_start()
+    total = of_p.near_total()
+    nodes = total[K : K + 1, :]
+    mean_p = total[0:K, :] / nodes
+    sum_g.over_z()
+    of_p.gather_far()
     loads[3].wait()
     link_copy.wait()
-    thin.gather_finish()
-    thin.products(tiles, col_ref, link)
-    wide.gather_near()
-    thin.place(link, thin_mean, weights)
-    wide.gather_far()
+    of_p.gather_finish()
+    of_p.products(tiles, col_ref, link, 0, SLOTS // 2)
+    of_r.gather_near()
+    of_p.products(tiles, col_ref, link, SLOTS // 2, SLOTS)
+    of_p.place(link, mean_p, weights)
+    of_x.gather_start()
+    sum_g.over_core()
     sum_g.share()
-    wide_mean = wide.near_total() / nodes
+    of_r.gather_far()
+    of_p.near()
+    of_r.gather_finish()
+    mean_r = of_r.near_total() / nodes
+    of_r.products(tiles, col_ref, link)
+    of_p.meet()
+    of_r.place(link, mean_r, weights)
+    of_x.gather_near()
+    mean_x = of_x.near_total() / nodes
+    of_x.gather_far()
+    of_r.near()
+    of_p.turn()
+    of_x.gather_finish()
+    of_x.products(tiles, col_ref, link)
+    of_x.place(link, mean_x, weights)
+    of_r.meet()
     weight_rows = [
-        jnp.transpose(wide_mean)[0:1, :],
-        jnp.transpose(jnp.concatenate([thin_mean, jnp.zeros((K, TILE), F32)], axis=0))[0:1, :],
+        jnp.transpose(jnp.concatenate([mean_x, mean_r], axis=0))[0:1, :],
+        jnp.transpose(jnp.concatenate([mean_p, jnp.zeros((K, TILE), F32)], axis=0))[0:1, :],
     ]
     for i in range(ROWS):
         weights[i, 8:9, :] = weight_rows[0]
@@ -524,35 +560,33 @@
     for o in range(1, ROWS):
         to = lax.rem(row + o, ROWS)
         here.send(weights.at[to], others.at[row], m_s, m_r, (to, col))
-    wide.gather_finish()
-    wide.products(tiles, col_ref, link, 0, SLOTS // 2)
-    thin.meet()
-    wide.products(tiles, col_ref, link, SLOTS // 2, SLOTS)
-    wide.place(link, wide_mean, weights)
     sum_g.finish()
     factor = Factor(sum_g.out, kinv)
     factor.first()
-    thin.turn()
+    of_x.near()
+    of_x.meet()
+    of_r.turn()
     factor.second()
-    wide.meet()
-    factor.third()
     wait_for(others.at[pl.ds(0, ROWS - 1)], m_r)
     means = jnp.concatenate([others[:, 8, :], others[:, 9, :]], axis=1)
     back = dot_tn(means, jnp.concatenate([others[:, b, :] for b in range(BLOCKS)], axis=1))
-    thin.finish(ast, 2 * K, scale, back)
-    wide.turn()
-    wide.finish(ast, 0, scale, back)
+    of_p.finish(ast, 2 * K, scale, back)
+    of_x.turn()
+    factor.third()
+    of_r.finish(ast, K, scale, back)
+    of_x.finish(ast, 0, scale, back)
     astv = ast[...]
     sum_h.pack(symmetric(dot_nt(stv, astv)))
     sum_h.start()
-    sum_h.over_col()
+    sum_h.over_z()
+    sum_h.over_core()
     sum_h.share()
     sum_h.finish()
 
     c_t, drop_t = ritz(sum_h.out, kinv[...])
     st2[K : 2 * K, :] = dot_nn(c_t, astv) - dot_nn(drop_t, stv)
     again.prepare(st2, K, scale)
-    again.gather_start()
+    again.gather_start_straight()
     cp_t = jnp.where(lax.broadcasted_iota(jnp.int32, (K, W3), 1) < K, 0.0, c_t)
     both = jnp.concatenate([c_t, cp_t], axis=0)
     moved = dot_nn(both, stv)
@@ -561,18 +595,19 @@
     stv2 = st2[...]
     sum_g2.pack(dot_nt(stv2, stv2))
     sum_g2.start()
+    sum_g2.over_z()
+    again.gather_pass()
+    again.gather_finish()
+    again.products(tiles, col_ref, link)
+    sum_g2.over_core()
+    sum_g2.share()
+    again.place(link)
     image = dot_nn(both, astv)
     ast2[0:K, :] = image[0:K, :]
     ast2[2 * K : W3, :] = image[K : 2 * K, :]
-    again.gather_near()
-    sum_g2.over_col()
-    again.gather_far()
-    again.gather_finish()
-    again.products(tiles, col_ref, link)
-    sum_g2.share()
-    again.place(link)
+    again.near()
+    again.meet()
     sum_g2.finish()
-    again.meet()
     factor = Factor(sum_g2.out, kinv)
     factor.first()
     factor.second()
@@ -585,7 +620,8 @@
         store.start()
     sum_h2.pack(symmetric(dot_nt(stv2, astv2)))
     sum_h2.start()
-    sum_h2.over_col()
+    sum_h2.over_z()
+    sum_h2.over_core()
     sum_h2.share()
     sum_h2.finish()
 
@@ -625,12 +661,13 @@
         scratch += [
             pltpu.VMEM((ROWS, 16, TILE), F32),
             pltpu.VMEM((ROWS, 16, TILE), F32),
-            pltpu.VMEM((COLS, 16, TILE), F32),
+            pltpu.VMEM((SIDE, 16, TILE), F32),
+            pltpu.VMEM((2, 16, TILE), F32),
             pltpu.VMEM((ROWS, 16, TILE), F32),
-            dma((3,)),
-            dma((3,)),
+            dma((4,)),
+            dma((4,)),
         ]
-    for width, extra in ((K, 16), (2 * K, 0), (K, 0)):
+    for width, extra in ((K, 16), (K, 0), (K, 0), (K, 0)):
         quarter = width // 4
         scratch += [
             pltpu.VMEM((COLS, BLOCKS, width + extra, TILE), BF16),

time: 148 us -> 149 us (level)
  no operation moved by 1% of the time
where the time goes in v3:
time: 149 us
  Pallas kernels  147 us (99%)
    pallas_call x1, Pallas kernels, whole_call(): pl.pallas_call(whole_kernel, name='iterations', out_shape=[jax.ShapeDtype...  135 us
    pallas_call x1, Pallas kernels, last_call(): pl.pallas_call(last_kernel, name='last_update', out_shape=[jax.ShapeDtype...  12.2 us

profile of v3, /device:TPU:1, one launch (start us, length us, event | category | flops | bytes accessed | tf_op | source)
XLA Modules:
  0.0 148.8 jit_solution(14848453119188445502)
XLA Ops:
  1.3 135.2 %iterations.1 = (f32[16,16,128]{2,1,0:T(8,128)}, f32[192,192]{1,0:T(8,128)}, f32[192,1024]{1,0:T(8,128)}, f32[192,1024]{1,0:T(8,128)}) custom-call(f32[64,1024]{1,0:T(8,128)} %bitcast.11, f32[64,1024]{1,0:T(8,128)} %bitcast.12, f32[64,1024]{1,0:T(8,128)} %bitcast.13, bf16[64,128,128]{2,1,0:T(8,128)(2,1)} %bitcast.10, s32[8,128]{1,0:T(8,128)} %bitcast.14, ...), custom_call_target="tpu_custom_call" | custom-call | tf_op jit(solution)/shard_map/iterations/pallas_call | solution.py:680
  136.5 12.2 %last_update.1 = (f32[64,1024]{1,0:T(8,128)}, f32[64,1024]{1,0:T(8,128)}, f32[64,1024]{1,0:T(8,128)}) custom-call(f32[16,16,128]{2,1,0:T(8,128)} %get-tuple-element.10.sums, f32[192,192]{1,0:T(8,128)} %get-tuple-element.11.kinv, f32[192,1024]{1,0:T(8,128)} %get-tuple-element.12.st_hbm, f32[192,1024]{1,0:T(8,128)} %get-tuple-element.13.ast_hbm), custom_call_target="tpu_custom_call" | custom-call | tf_op jit(solution)/shard_map/last_update/pallas_call | solution.py:715
